TPU v7x, 32 devices: a whole 2x2x4 slice. The times are simulated.
32 devices in a mesh: outer: 2 (over y), rep: 4 (over x, core), tp: 4 (over z).
Axes of the slice: x: 2, y: 2, z: 4, core: 2. Of those that a mesh axis runs over, the one named last changes fastest.
Arguments:
- hidden: bfloat16 [16384, 8192], P(('outer', 'rep'), 'tp'), parts along dimension 0, may hold values from -2000 to 2000, as said below
- lengths: int32 [8], P('outer'), parts along dimension 0, may hold values from 1 to 16, 32 in all
- adapter_index: int32 [8], P('outer'), parts along dimension 0, may hold values from 0 to 3, as said below
- gain: float32 [8192], P('tp'), may hold values from 0.1 to 1.9
- wkv: bfloat16 [8192, 2048], P('tp'), may hold values from -0.09375 to 0.09375
- down_weights: bfloat16 [8192, 128], P('tp'), may hold values from -0.0625 to 0.0625
- key_up_weights: bfloat16 [64, 1024], replicated, may hold values from -1.5 to 1.5
- value_up_weights: bfloat16 [64, 1024], replicated, may hold values from -1.5 to 1.5
Outputs:
- kv_cache: bfloat16 [16384, 2048], P(('outer', 'rep'), 'tp'), parts along dimension 0
There are 2 independent parts, one for each index of `outer`. A program takes and returns all parts, laid end to end along the dimension named above; an argument that names none is the same for every part. Nothing has to cross between parts.
Inputs may be any that keep to these rules, and one draw needn't show every extreme that they name: `hidden`: the layer's input activations. The lengths sum to exactly 32, and some owner fills all 16 slots. `adapter_index`: every adapter is named by some owner.
All inputs are finite; a program needn't handle non-finite values.
Results may differ from a plain program's by a relative error of at most 0.012.
Values may be sent and summed in bfloat16 or wider, within the bound.
A program may use at most 128 MiB of HBM per device.

v0:
```python
import functools

import jax
import jax.numpy as jnp
from jax import lax
from jax.experimental import pallas as pl
from jax.experimental.pallas import tpu as pltpu
from jax.sharding import PartitionSpec as P

MODEL_WIDTH = 8192
KEY_VALUE_HEADS = 8
HEAD_WIDTH = 128
SPAN = 128
ADAPTER_RANK = 16
SLOTS = 16

EPSILON = 1e-05
THETA = 500000.0
ADAPTER_SCALE = 0.5


def rotate_keys(keys, positions):
    head_size = keys.shape[-1]
    half = head_size // 2
    index = jnp.arange(half, dtype=jnp.float32)
    inverse = jnp.power(jnp.float32(THETA), -2.0 * index / head_size)
    angles = positions.astype(jnp.float32)[:, None] * inverse[None, :]
    cosine = jnp.concatenate([jnp.cos(angles), jnp.cos(angles)], axis=1)
    sine = jnp.concatenate([jnp.sin(angles), jnp.sin(angles)], axis=1)
    turned = jnp.concatenate([-keys[..., half:], keys[..., :half]], axis=-1)
    return keys * cosine[:, None, :] + turned * sine[:, None, :]


def kernel(
    n, blocks, rows, columns,
    hidden, gain, wkv, down, up, summed, square_sums,
    scaled, partial, from_left, from_right, squares,
    right_send, right_recv, left_send, left_recv, square_send, square_recv,
):
    me = lax.axis_index("tp")
    right, left = lax.rem(me + 1, n), lax.rem(me + n - 1, n)
    mesh_id = pl.DeviceIdType.MESH

    barrier = pltpu.get_barrier_semaphore()

    @pl.loop(0, n)
    def _(peer):
        @pl.when(peer != me)
        def _():
            pl.semaphore_signal(barrier, inc=1, device_id={"tp": peer}, device_id_type=mesh_id)

    pl.semaphore_wait(barrier, n - 1)

    def rightward(b, j):
        return pltpu.make_async_remote_copy(
            src_ref=partial.at[b, j], dst_ref=from_left.at[b, j],
            send_sem=right_send.at[b, j], recv_sem=right_recv.at[b, j],
            device_id={"tp": right}, device_id_type=mesh_id,
        )

    def leftward(b, j):
        return pltpu.make_async_remote_copy(
            src_ref=partial.at[b, j], dst_ref=from_right.at[b, j],
            send_sem=left_send.at[b, j], recv_sem=left_recv.at[b, j],
            device_id={"tp": left}, device_id_type=mesh_id,
        )

    def square_copy(source, peer):
        return pltpu.make_async_remote_copy(
            src_ref=squares.at[source], dst_ref=squares.at[source],
            send_sem=square_send.at[peer], recv_sem=square_recv.at[source],
            device_id={"tp": peer}, device_id_type=mesh_id,
        )

    def add_arrived(b, j, arrived):
        partial[b, j] = (
            partial[b, j].astype(jnp.float32) + arrived[b, j].astype(jnp.float32)
        ).astype(jnp.bfloat16)

    ones = jnp.ones((8, hidden.shape[1]), jnp.bfloat16)
    over_width = (((1,), (1,)), ((), ()))

    @pl.loop(0, blocks)
    def _(b):
        values = hidden[pl.ds(b * rows, rows), :].astype(jnp.float32)
        scaled[...] = (values * gain[...]).astype(jnp.bfloat16)
        square = values * values
        high = square.astype(jnp.bfloat16)
        low = (square - high.astype(jnp.float32)).astype(jnp.bfloat16)
        squares[me, :, pl.ds(b * rows, rows)] = lax.dot_general(
            ones, high, over_width, preferred_element_type=jnp.float32
        ) + lax.dot_general(ones, low, over_width, preferred_element_type=jnp.float32)
        low_rank = jnp.dot(
            scaled[...], down[...], preferred_element_type=jnp.float32
        ).astype(jnp.bfloat16)

        @pl.loop(0, n)
        def _(j):
            here = pl.ds(pl.multiple_of(j * columns, columns), columns)
            base = jnp.dot(scaled[...], wkv[:, here], preferred_element_type=jnp.float32)
            delta = jnp.dot(low_rank, up[:, here], preferred_element_type=jnp.float32)
            partial[b, j] = (base + ADAPTER_SCALE * delta).astype(jnp.bfloat16)

        @pl.when(me == 0)
        def _():
            @pl.loop(1, n)
            def _(j):
                rightward(b, n - j).start()

        @pl.when(me == n - 1)
        def _():
            @pl.loop(0, n - 1)
            def _(j):
                leftward(b, j).start()

    @pl.loop(0, n)
    def _(peer):
        @pl.when(peer != me)
        def _():
            square_copy(me, peer).start()

    @pl.loop(0, blocks + 1)
    def _(step):
        @pl.when(step < blocks)
        def _():
            b = step

            @pl.when((me > 0) & (me < n - 1))
            def _():
                @pl.loop(0, n)
                def _(i):
                    j = n - 1 - i

                    @pl.when(j > me)
                    def _():
                        rightward(b, j).wait_recv()
                        add_arrived(b, j, from_left)
                        rightward(b, j).start()

                    @pl.when(i < me)
                    def _():
                        leftward(b, i).wait_recv()
                        add_arrived(b, i, from_right)
                        leftward(b, i).start()

        @pl.when(step > 0)
        def _():
            b = step - 1

            @pl.when(me > 0)
            def _():
                rightward(b, me).wait_recv()
                add_arrived(b, me, from_left)

            @pl.when(me < n - 1)
            def _():
                leftward(b, me).wait_recv()
                add_arrived(b, me, from_right)

            summed[pl.ds(b * rows, rows), :] = partial[b, me]

    @pl.loop(0, n)
    def _(peer):
        @pl.when(peer != me)
        def _():
            square_copy(peer, peer).wait_recv()
            square_copy(me, peer).wait_send()

    total = squares[0]
    for peer in range(1, n):
        total = total + squares[peer]
    square_sums[...] = total

    @pl.loop(0, blocks)
    def _(b):
        @pl.loop(0, n)
        def _(j):
            @pl.when(j > me)
            def _():
                rightward(b, j).wait_send()

            @pl.when(j < me)
            def _():
                leftward(b, j).wait_send()


def body(hidden, lengths, adapter_index, gain, wkv, down_weights, key_up_weights, value_up_weights):
    my_replica = lax.axis_index("rep")
    my_shard = lax.axis_index("tp")
    n = lax.axis_size("tp")
    own_length = lengths[my_replica]
    adapter = adapter_index[my_replica]
    key_columns = key_up_weights.shape[1]
    width = hidden.shape[1]
    row_count = hidden.shape[0]
    columns = wkv.shape[1] // n
    adapters = key_up_weights.shape[0] // ADAPTER_RANK
    mine = (jnp.arange(adapters) == adapter)[:, None, None]
    key_up = jnp.where(mine, key_up_weights.reshape(adapters, ADAPTER_RANK, -1), 0)
    value_up = jnp.where(mine, value_up_weights.reshape(adapters, ADAPTER_RANK, -1), 0)
    up = jnp.concatenate(
        [
            jnp.concatenate([key_up, jnp.zeros_like(value_up)], axis=2),
            jnp.concatenate([jnp.zeros_like(key_up), value_up], axis=2),
        ],
        axis=1,
    ).reshape(down_weights.shape[1], wkv.shape[1])
    rows = 2 * SPAN
    blocks = row_count // rows
    vmem = pl.BlockSpec(memory_space=pltpu.VMEM)
    chunk_buffer = pltpu.VMEM((blocks, n, rows, columns), jnp.bfloat16)
    chunk_semaphores = pltpu.SemaphoreType.DMA((blocks, n))
    summed, square_sums = pl.pallas_call(
        functools.partial(kernel, n, blocks, rows, columns),
        out_shape=(
            jax.ShapeDtypeStruct((row_count, columns), jnp.bfloat16),
            jax.ShapeDtypeStruct((8, row_count), jnp.float32),
        ),
        in_specs=[vmem] * 5,
        out_specs=(vmem, vmem),
        scratch_shapes=[
            pltpu.VMEM((rows, width), jnp.bfloat16),
            chunk_buffer,
            chunk_buffer,
            chunk_buffer,
            pltpu.VMEM((n, 8, row_count), jnp.float32),
            chunk_semaphores,
            chunk_semaphores,
            chunk_semaphores,
            chunk_semaphores,
            pltpu.SemaphoreType.DMA((n,)),
            pltpu.SemaphoreType.DMA((n,)),
        ],
        compiler_params=pltpu.CompilerParams(
            collective_id=0, has_side_effects=True, vmem_limit_bytes=60 * 1024 * 1024
        ),
    )(hidden, gain[None, :], wkv, down_weights, up)
    inverse_rms = lax.rsqrt(square_sums[0] / MODEL_WIDTH + EPSILON)
    normed = summed.astype(jnp.float32) * inverse_rms[:, None]
    positions = jnp.arange(row_count, dtype=jnp.int32)
    turned = rotate_keys(
        normed.reshape(row_count, columns // HEAD_WIDTH, HEAD_WIDTH), positions
    ).reshape(row_count, columns)
    is_key = my_shard * columns < key_columns
    live = positions < own_length * SPAN
    result = jnp.where(is_key, turned, normed)
    return jnp.where(live[:, None], result, 0.0).astype(jnp.bfloat16)


def solution(mesh):
    return jax.shard_map(
        body,
        mesh=mesh,
        in_specs=(
            P(("outer", "rep"), "tp"),
            P("outer"),
            P("outer"),
            P("tp"),
            P("tp", None),
            P("tp", None),
            P(),
            P(),
        ),
        out_specs=P(("outer", "rep"), "tp"),
        check_vma=False,
    )
```

profile of v0, /device:TPU:0, one launch (start us, length us, event | category | flops | bytes accessed | tf_op | source)
XLA Modules:
  0.0 212.1 jit_solution(3906085709719036647)
XLA Ops:
  0.0 1.2 dynamic_slice.7
  1.2 0.6 iota_compare_fusion.3
  1.9 1.1 broadcast_select_fusion.1
  3.0 0.8 fusion.5
  3.8 175.1 %shard_map.82 = (bf16[2048,512]{1,0:T(8,128)(2,1)}, f32[8,2048]{1,0:T(8,128)}) custom-call(bf16[2048,2048]{1,0:T(8,128)(2,1)} %hidden.1, f32[1,2048]{1,0:T(1,128)} %bitcast.28, bf16[2048,2048]{1,0:T(8,128)(2,1)} %wkv.1, bf16[2048,128]{1,0:T(8,128)(2,1)} %down.1, bf16[128,2048]{1,0:T(8,128)(2,1)} %bitcast.23), custom_call_target="tpu_custom_call" | custom-call | tf_op jit(solution)/shard_map/pallas_call | solution.py:213
  178.8 0.9 add_rsqrt_fusion
  179.7 3.9 %convert_multiply_fusion = f32[2048,512]{1,0:T(8,128)} fusion(bf16[2048,512]{1,0:T(8,128)(2,1)} %get-tuple-element.7, f32[2048]{0:T(1024)S(1)} %bitcast.26), kind=kLoop, calls=%fused_computation.7 | loop fusion | flops 2097152 | bytes 6299648 | tf_op jit(solution)/shard_map/mul | solution.py:239
  183.6 5.3 %reshape.53 = f32[2048,4,128]{2,1,0:T(4,128)} reshape(f32[2048,512]{1,0:T(8,128)} %convert_multiply_fusion) | data formatting | bytes 8388608 | tf_op jit(solution)/shard_map/reshape | solution.py:242
  188.9 5.8 %slice_negate_fusion = (f32[2048,4,64]{2,1,0:T(4,128)S(1)}, f32[2048,4,64]{2,1,0:T(4,128)S(1)}) fusion(f32[2048,4,128]{2,1,0:T(4,128)} %reshape.53), kind=kLoop, calls=%fused_computation.5 | loop fusion | flops 524288 | bytes 8388608 | tf_op jit(solution)/shard_map/neg | solution.py:30
  194.7 3.7 %multiply_cosine_fusion = (f32[2048,64]{1,0:T(8,128)S(1)}, f32[2048,64]{1,0:T(8,128)S(1)}) fusion(f32[64]{0:T(128)S(1)} %multiply_power_fusion, f32[2048]{0:T(1024)S(1)} %iota_convert_fusion), kind=kLoop, calls=%fused_computation.9 | loop fusion | flops 131072 | bytes 1057024 | tf_op jit(solution)/shard_map/cos | solution.py:28
  198.4 0.6 pad_maximum_fusion
  199.0 0.0 copy-start.1
  199.0 3.8 %maximum_multiply_fusion = f32[2048,4,128]{2,1,0:T(4,128)} fusion(f32[2048,4,64]{2,1,0:T(4,128)S(1)} %get-tuple-element.10, f32[2048,4,64]{2,1,0:T(4,128)S(1)} %get-tuple-element.9, f32[2048,128]{1,0:T(8,128)S(1)} %get-tuple-element.16), kind=kLoop, calls=%fused_computation.6 | loop fusion | flops 2097152 | bytes 9437184 | tf_op jit(solution)/shard_map/mul | solution.py:31
  202.8 0.0 copy-start
  202.8 0.0 copy-done.1
  202.8 0.6 dynamic_slice.6
  204.1 2.4 %mul.82 = f32[2048,4,128]{2,1,0:T(4,128)} broadcast(f32[2048,128]{1,0:T(8,128)S(1)} %get-tuple-element.15), dimensions={0,2} | broadcast | bytes 5242880 | tf_op jit(solution)/shard_map/mul | solution.py:31
  206.5 0.0 copy-done
  206.5 5.7 %fusion.2 = bf16[2048,512]{1,0:T(8,128)(2,1)} fusion(f32[256,8,4,128]{3,2,1,0:T(4,128)} %bitcast.22, f32[256,8,4,128]{3,2,1,0:T(4,128)} %bitcast.21, pred[2048]{0:T(1024)(128)(4,1)S(1)} %iota_compare_fusion.2, pred[]{:T(512)S(6)} %lt.20, f32[2048]{0:T(1024)S(1)} %bitcast.27, bf16[2048,512]{1,0:T(8,128)(2,1)S(1)} %copy-done), kind=kLoop, calls=%fused_computation.3 | loop fusion | flops 7340032 | bytes 12593153 | tf_op jit(solution)/shard_map/convert_element_type | solution.py:247
  (3 shorter events, 0.0 us)
Async XLA Ops:
  199.0 3.8 %copy-start.1 = (s32[4]{0:T(128)S(1)}, s32[4]{0:T(128)}, u32[]{:S(2)}) copy-start(s32[4]{0:T(128)} %param.9) | copy-start | bytes 52
  202.8 3.7 %copy-start = (bf16[2048,512]{1,0:T(8,128)(2,1)S(1)}, bf16[2048,512]{1,0:T(8,128)(2,1)}, u32[]{:S(2)}) copy-start(bf16[2048,512]{1,0:T(8,128)(2,1)} %get-tuple-element.7) | copy-start | bytes 6291460
where the time goes:
time: 212 us
  Pallas kernels  175 us (83%)
  other arithmetic  26.9 us (13%)
  local copies, waits for them, and re-layouts  9.45 us (4%)
    pallas_call x1, Pallas kernels, body(): pl.pallas_call(functools.partial(kernel, n, blocks, rows, columns), out_s...  175 us
    neg x1, other arithmetic, rotate_keys(): turned = jnp.concatenate([-keys[..., half:], keys[..., :half]], axis=-1)  5.79 us
    convert_element_type x1, other arithmetic, body(): return jnp.where(live[:, None], result, 0.0).astype(jnp.bfloat16)  5.68 us
    reshape x1, local copies, waits for them, and re-layouts, body(): normed.reshape(row_count, columns // HEAD_WIDTH, HEAD_WIDTH)  5.27 us

commit v1 on v0

--- a/solution.py
+++ b/solution.py
@@ -19,22 +19,9 @@
 ADAPTER_SCALE = 0.5
 
 
-def rotate_keys(keys, positions):
-    head_size = keys.shape[-1]
-    half = head_size // 2
-    index = jnp.arange(half, dtype=jnp.float32)
-    inverse = jnp.power(jnp.float32(THETA), -2.0 * index / head_size)
-    angles = positions.astype(jnp.float32)[:, None] * inverse[None, :]
-    cosine = jnp.concatenate([jnp.cos(angles), jnp.cos(angles)], axis=1)
-    sine = jnp.concatenate([jnp.sin(angles), jnp.sin(angles)], axis=1)
-    turned = jnp.concatenate([-keys[..., half:], keys[..., :half]], axis=-1)
-    return keys * cosine[:, None, :] + turned * sine[:, None, :]
-
-
 def kernel(
-    n, blocks, rows, columns,
-    hidden, gain, wkv, down, up, summed, square_sums,
-    scaled, partial, from_left, from_right, squares,
+    n, blocks, rows, columns, key_columns,
+    hidden, gain, wkv, down, up, frequency, limit, result, scaled, cosine, sine, partial, from_left, from_right, squares,
     right_send, right_recv, left_send, left_recv, square_send, square_recv,
 ):
     me = lax.axis_index("tp")
@@ -124,6 +111,15 @@
         @pl.when(step < blocks)
         def _():
             b = step
+            here = pl.ds(b * rows, rows)
+            place = lax.broadcasted_iota(jnp.int32, (rows, HEAD_WIDTH), 0) + b * rows
+            lane = lax.broadcasted_iota(jnp.int32, (rows, HEAD_WIDTH), 1)
+            angles = place.astype(jnp.float32) * frequency[...]
+            is_key = me * columns < key_columns
+            cosine[here, :] = jnp.where(is_key, jnp.cos(angles), 1.0)
+            turn = jnp.sin(angles)
+            turn = jnp.where(lane < HEAD_WIDTH // 2, -turn, turn)
+            sine[here, :] = jnp.where(is_key, turn, 0.0)
 
             @pl.when((me > 0) & (me < n - 1))
             def _():
@@ -157,8 +153,6 @@
                 leftward(b, me).wait_recv()
                 add_arrived(b, me, from_right)
 
-            summed[pl.ds(b * rows, rows), :] = partial[b, me]
-
     @pl.loop(0, n)
     def _(peer):
         @pl.when(peer != me)
@@ -166,10 +160,21 @@
             square_copy(peer, peer).wait_recv()
             square_copy(me, peer).wait_send()
 
-    total = squares[0]
-    for peer in range(1, n):
-        total = total + squares[peer]
-    square_sums[...] = total
+    @pl.loop(0, blocks)
+    def _(b):
+        here = pl.ds(b * rows, rows)
+        total = squares[0, :, here]
+        for peer in range(1, n):
+            total = total + squares[peer, :, here]
+        inverse_rms = jnp.transpose(lax.rsqrt(total / MODEL_WIDTH + EPSILON))[:, 0:1]
+        place = lax.broadcasted_iota(jnp.int32, (rows, HEAD_WIDTH), 0) + b * rows
+        live = place < limit[...]
+        for head in range(columns // HEAD_WIDTH):
+            own = slice(head * HEAD_WIDTH, (head + 1) * HEAD_WIDTH)
+            normed = partial[b, me, :, own].astype(jnp.float32) * inverse_rms
+            turned = pltpu.roll(normed, HEAD_WIDTH // 2, 1)
+            rotated = normed * cosine[here, :] + turned * sine[here, :]
+            result[here, own] = jnp.where(live, rotated, 0.0).astype(jnp.bfloat16)
 
     @pl.loop(0, blocks)
     def _(b):
@@ -186,7 +191,6 @@
 
 def body(hidden, lengths, adapter_index, gain, wkv, down_weights, key_up_weights, value_up_weights):
     my_replica = lax.axis_index("rep")
-    my_shard = lax.axis_index("tp")
     n = lax.axis_size("tp")
     own_length = lengths[my_replica]
     adapter = adapter_index[my_replica]
@@ -210,16 +214,18 @@
     vmem = pl.BlockSpec(memory_space=pltpu.VMEM)
     chunk_buffer = pltpu.VMEM((blocks, n, rows, columns), jnp.bfloat16)
     chunk_semaphores = pltpu.SemaphoreType.DMA((blocks, n))
-    summed, square_sums = pl.pallas_call(
-        functools.partial(kernel, n, blocks, rows, columns),
-        out_shape=(
-            jax.ShapeDtypeStruct((row_count, columns), jnp.bfloat16),
-            jax.ShapeDtypeStruct((8, row_count), jnp.float32),
-        ),
-        in_specs=[vmem] * 5,
-        out_specs=(vmem, vmem),
+    index = jnp.arange(HEAD_WIDTH // 2, dtype=jnp.float32)
+    frequency = jnp.tile(jnp.power(jnp.float32(THETA), -2.0 * index / HEAD_WIDTH), 2)[None, :]
+    limit = jnp.full((1, HEAD_WIDTH), own_length * SPAN, jnp.int32)
+    return pl.pallas_call(
+        functools.partial(kernel, n, blocks, rows, columns, key_columns),
+        out_shape=jax.ShapeDtypeStruct((row_count, columns), jnp.bfloat16),
+        in_specs=[vmem] * 7,
+        out_specs=vmem,
         scratch_shapes=[
             pltpu.VMEM((rows, width), jnp.bfloat16),
+            pltpu.VMEM((row_count, HEAD_WIDTH), jnp.float32),
+            pltpu.VMEM((row_count, HEAD_WIDTH), jnp.float32),
             chunk_buffer,
             chunk_buffer,
             chunk_buffer,
@@ -234,17 +240,7 @@
         compiler_params=pltpu.CompilerParams(
             collective_id=0, has_side_effects=True, vmem_limit_bytes=60 * 1024 * 1024
         ),
-    )(hidden, gain[None, :], wkv, down_weights, up)
-    inverse_rms = lax.rsqrt(square_sums[0] / MODEL_WIDTH + EPSILON)
-    normed = summed.astype(jnp.float32) * inverse_rms[:, None]
-    positions = jnp.arange(row_count, dtype=jnp.int32)
-    turned = rotate_keys(
-        normed.reshape(row_count, columns // HEAD_WIDTH, HEAD_WIDTH), positions
-    ).reshape(row_count, columns)
-    is_key = my_shard * columns < key_columns
-    live = positions < own_length * SPAN
-    result = jnp.where(is_key, turned, normed)
-    return jnp.where(live[:, None], result, 0.0).astype(jnp.bfloat16)
+    )(hidden, gain[None, :], wkv, down_weights, up, frequency, limit)
 
 
 def solution(mesh):

time: 212 us -> 188 us (0.89)
  other arithmetic: 26.9 us -> 2.55 us
  Pallas kernels: 175 us -> 178 us
  local copies, waits for them, and re-layouts: 9.45 us -> 6.68 us
    mul x2 -> x0, other arithmetic: 7.69 us -> none  [the longest x1 3.89 us: body(): normed = summed.astype(jnp.float32) * inverse_rms[:, None]]
    neg x1 -> x0, other arithmetic: 5.79 us -> none  [rotate_keys(): turned = jnp.concatenate([-keys[..., half:], keys[..., :half]], axis=-1)]
    convert_element_type x2 -> x0, other arithmetic: 5.68 us -> none  [the longest x1 5.68 us: body(): return jnp.where(live[:, None], result, 0.0).astype(jnp.bfloat16)]
    reshape x1 -> x0, local copies, waits for them, and re-layouts: 5.27 us -> none  [body(): normed.reshape(row_count, columns // HEAD_WIDTH, HEAD_WIDTH)]
    cos x1 -> x0, other arithmetic: 3.69 us -> none  [rotate_keys(): cosine = jnp.concatenate([jnp.cos(angles), jnp.cos(angles)], axis=1)]
    pallas_call x1, Pallas kernels: 175 us -> 178 us  [body(): pl.pallas_call(functools.partial(kernel, n, blocks, rows, columns, key_co...]
    unnamed x4 -> x1, local copies, waits for them, and re-layouts: 0.01 us -> 3.05 us
    mul x1 -> x0, local copies, waits for them, and re-layouts: 2.35 us -> none  [rotate_keys(): return keys * cosine[:, None, :] + turned * sine[:, None, :]]
where the time goes in v1:
time: 188 us
  Pallas kernels  178 us (95%)
  local copies, waits for them, and re-layouts  6.68 us (4%)
  other arithmetic  2.55 us (1%)
    pallas_call x1, Pallas kernels, body(): pl.pallas_call(functools.partial(kernel, n, blocks, rows, columns, key_co...  178 us

profile of v1, /device:TPU:0, one launch (start us, length us, event | category | flops | bytes accessed | tf_op | source)
XLA Modules:
  0.0 188.3 jit_solution(15184058180525724760)
XLA Ops:
  0.0 1.2 dynamic_slice.6
  1.2 0.6 iota_compare_fusion.2
  1.9 1.2 dynamic_slice.7
  3.8 0.5 broadcast_in_dim.26.limit
  4.3 0.6 broadcast_in_dim_tile.3.frequency
  5.0 1.1 broadcast_select_fusion.1
  6.0 0.8 fusion.2
  6.8 178.4 %shard_map.82 = bf16[2048,512]{1,0:T(8,128)(2,1)} custom-call(bf16[2048,2048]{1,0:T(8,128)(2,1)} %hidden.1, f32[1,2048]{1,0:T(1,128)} %bitcast.9, bf16[2048,2048]{1,0:T(8,128)(2,1)} %wkv.1, bf16[2048,128]{1,0:T(8,128)(2,1)} %down.1, bf16[128,2048]{1,0:T(8,128)(2,1)} %bitcast.6, f32[1,128]{1,0:T(1,128)} %broadcast_in_dim_tile.3.frequency, ...), custom_call_target="tpu_custom_call" | custom-call | tf_op jit(solution)/shard_map/pallas_call | solution.py:220
  185.2 3.0 %copy.10 = bf16[2048,512]{1,0:T(8,128)(2,1)} copy(bf16[2048,512]{1,0:T(8,128)(2,1)} %shard_map.82) | data formatting | bytes 4194304
  (2 shorter events, 0.0 us)

commit v2 on v1

--- a/solution.py
+++ b/solution.py
@@ -67,8 +67,7 @@
     ones = jnp.ones((8, hidden.shape[1]), jnp.bfloat16)
     over_width = (((1,), (1,)), ((), ()))
 
-    @pl.loop(0, blocks)
-    def _(b):
+    def compute(b):
         values = hidden[pl.ds(b * rows, rows), :].astype(jnp.float32)
         scaled[...] = (values * gain[...]).astype(jnp.bfloat16)
         square = values * values
@@ -100,14 +99,24 @@
             def _(j):
                 leftward(b, j).start()
 
-    @pl.loop(0, n)
-    def _(peer):
-        @pl.when(peer != me)
-        def _():
-            square_copy(me, peer).start()
-
-    @pl.loop(0, blocks + 1)
+    early = blocks // 2
+
+    @pl.loop(0, blocks + early)
     def _(step):
+        @pl.when(step < early)
+        def _():
+            @pl.loop(0, 2)
+            def _(which):
+                compute(2 * step + which)
+
+        @pl.when(step == early - 1)
+        def _():
+            @pl.loop(0, n)
+            def _(peer):
+                @pl.when(peer != me)
+                def _():
+                    square_copy(me, peer).start()
+
         @pl.when(step < blocks)
         def _():
             b = step
@@ -139,9 +148,9 @@
                         add_arrived(b, i, from_right)
                         leftward(b, i).start()
 
-        @pl.when(step > 0)
-        def _():
-            b = step - 1
+        @pl.when(step >= early)
+        def _():
+            b = step - early
 
             @pl.when(me > 0)
             def _():

time: 188 us -> 179 us (0.952)
  Pallas kernels: 178 us -> 169 us
    pallas_call x1, Pallas kernels: 178 us -> 169 us  [body(): pl.pallas_call(functools.partial(kernel, n, blocks, rows, columns, key_co...]
where the time goes in v2:
time: 179 us
  Pallas kernels  169 us (94%)
  local copies, waits for them, and re-layouts  6.68 us (4%)
  other arithmetic  2.55 us (1%)
    pallas_call x1, Pallas kernels, body(): pl.pallas_call(functools.partial(kernel, n, blocks, rows, columns, key_co...  169 us

profile of v2, /device:TPU:0, one launch (start us, length us, event | category | flops | bytes accessed | tf_op | source)
XLA Modules:
  0.0 179.2 jit_solution(167406956003718237)
XLA Ops:
  0.0 1.2 dynamic_slice.6
  1.2 0.6 iota_compare_fusion.2
  1.9 1.2 dynamic_slice.7
  3.8 0.5 broadcast_in_dim.26.limit
  4.3 0.6 broadcast_in_dim_tile.3.frequency
  5.0 1.1 broadcast_select_fusion.1
  6.0 0.8 fusion.2
  6.8 169.3 %shard_map.82 = bf16[2048,512]{1,0:T(8,128)(2,1)} custom-call(bf16[2048,2048]{1,0:T(8,128)(2,1)} %hidden.1, f32[1,2048]{1,0:T(1,128)} %bitcast.9, bf16[2048,2048]{1,0:T(8,128)(2,1)} %wkv.1, bf16[2048,128]{1,0:T(8,128)(2,1)} %down.1, bf16[128,2048]{1,0:T(8,128)(2,1)} %bitcast.6, f32[1,128]{1,0:T(1,128)} %broadcast_in_dim_tile.3.frequency, ...), custom_call_target="tpu_custom_call" | custom-call | tf_op jit(solution)/shard_map/pallas_call | solution.py:229
  176.1 3.0 %copy.10 = bf16[2048,512]{1,0:T(8,128)(2,1)} copy(bf16[2048,512]{1,0:T(8,128)(2,1)} %shard_map.82) | data formatting | bytes 4194304
  (2 shorter events, 0.0 us)

commit v3 on v2

--- a/solution.py
+++ b/solution.py
@@ -67,37 +67,38 @@
     ones = jnp.ones((8, hidden.shape[1]), jnp.bfloat16)
     over_width = (((1,), (1,)), ((), ()))
 
+    is_first = (n - 1 - me) // (n - 1)
+
     def compute(b):
         values = hidden[pl.ds(b * rows, rows), :].astype(jnp.float32)
         scaled[...] = (values * gain[...]).astype(jnp.bfloat16)
+        low_rank = jnp.dot(
+            scaled[...], down[...], preferred_element_type=jnp.float32
+        ).astype(jnp.bfloat16)
+
+        @pl.loop(0, n)
+        def _(i):
+            j = i + is_first * (n - 1 - 2 * i)
+            here = pl.ds(pl.multiple_of(j * columns, columns), columns)
+            base = jnp.dot(scaled[...], wkv[:, here], preferred_element_type=jnp.float32)
+            delta = jnp.dot(low_rank, up[:, here], preferred_element_type=jnp.float32)
+            partial[b, j] = (base + ADAPTER_SCALE * delta).astype(jnp.bfloat16)
+
+            @pl.when((me == 0) & (j > 0))
+            def _():
+                rightward(b, j).start()
+
+            @pl.when((me == n - 1) & (j < n - 1))
+            def _():
+                leftward(b, j).start()
+
+        values = hidden[pl.ds(b * rows, rows), :].astype(jnp.float32)
         square = values * values
         high = square.astype(jnp.bfloat16)
         low = (square - high.astype(jnp.float32)).astype(jnp.bfloat16)
         squares[me, :, pl.ds(b * rows, rows)] = lax.dot_general(
             ones, high, over_width, preferred_element_type=jnp.float32
         ) + lax.dot_general(ones, low, over_width, preferred_element_type=jnp.float32)
-        low_rank = jnp.dot(
-            scaled[...], down[...], preferred_element_type=jnp.float32
-        ).astype(jnp.bfloat16)
-
-        @pl.loop(0, n)
-        def _(j):
-            here = pl.ds(pl.multiple_of(j * columns, columns), columns)
-            base = jnp.dot(scaled[...], wkv[:, here], preferred_element_type=jnp.float32)
-            delta = jnp.dot(low_rank, up[:, here], preferred_element_type=jnp.float32)
-            partial[b, j] = (base + ADAPTER_SCALE * delta).astype(jnp.bfloat16)
-
-        @pl.when(me == 0)
-        def _():
-            @pl.loop(1, n)
-            def _(j):
-                rightward(b, n - j).start()
-
-        @pl.when(me == n - 1)
-        def _():
-            @pl.loop(0, n - 1)
-            def _(j):
-                leftward(b, j).start()
 
     early = blocks // 2
 

time: 179 us -> 176 us (0.983)
  Pallas kernels: 169 us -> 166 us
    pallas_call x1, Pallas kernels: 169 us -> 166 us  [body(): pl.pallas_call(functools.partial(kernel, n, blocks, rows, columns, key_co...]
where the time goes in v3:
time: 176 us
  Pallas kernels  166 us (94%)
  local copies, waits for them, and re-layouts  6.68 us (4%)
  other arithmetic  2.55 us (1%)
    pallas_call x1, Pallas kernels, body(): pl.pallas_call(functools.partial(kernel, n, blocks, rows, columns, key_co...  166 us

profile of v3, /device:TPU:0, one launch (start us, length us, event | category | flops | bytes accessed | tf_op | source)
XLA Modules:
  0.0 175.9 jit_solution(18236215533028982845)
XLA Ops:
  0.0 1.2 dynamic_slice.6
  1.2 0.6 iota_compare_fusion.2
  1.9 1.2 dynamic_slice.7
  3.8 0.5 broadcast_in_dim.26.limit
  4.3 0.6 broadcast_in_dim_tile.3.frequency
  5.0 1.1 broadcast_select_fusion.1
  6.0 0.8 fusion.2
  6.8 166.0 %shard_map.82 = bf16[2048,512]{1,0:T(8,128)(2,1)} custom-call(bf16[2048,2048]{1,0:T(8,128)(2,1)} %hidden.1, f32[1,2048]{1,0:T(1,128)} %bitcast.9, bf16[2048,2048]{1,0:T(8,128)(2,1)} %wkv.1, bf16[2048,128]{1,0:T(8,128)(2,1)} %down.1, bf16[128,2048]{1,0:T(8,128)(2,1)} %bitcast.6, f32[1,128]{1,0:T(1,128)} %broadcast_in_dim_tile.3.frequency, ...), custom_call_target="tpu_custom_call" | custom-call | tf_op jit(solution)/shard_map/pallas_call | solution.py:230
  172.9 3.0 %copy.10 = bf16[2048,512]{1,0:T(8,128)(2,1)} copy(bf16[2048,512]{1,0:T(8,128)(2,1)} %shard_map.82) | data formatting | bytes 4194304
  (2 shorter events, 0.0 us)
